TPU v7x, 256 devices: a whole 4x4x8 slice. The times are simulated.
256 devices in a mesh: grp: 8 (over z), lvl: 32 (over x, y, core).
Axes of the slice: x: 4, y: 4, z: 8, core: 2. Of those that a mesh axis runs over, the one named last changes fastest.
Arguments:
- vectors: bfloat16 [524288, 384], P(('grp', 'lvl')), may hold values from -6 to 6
- leaf_in: bfloat16 [256, 524288], P(None, ('grp', 'lvl')), may hold values from -0.125 to 0.125
- leaf_out: bfloat16 [524288, 256], P(('grp', 'lvl')), may hold values from -0.375 to 0.375
- factors: bfloat16 [256, 8, 2, 256, 256], P(('grp', 'lvl')), may hold values from -0.25 to 0.25
- dense_rows: bfloat16 [1536, 524288], P(None, ('grp', 'lvl')), may hold values from -0.03125 to 0.03125
- sample_rows: int32 [1536], P(('grp', 'lvl')), may hold values from 0 to 2047
Outputs:
- residual: float32 [1536, 384], P(('grp', 'lvl'))
Inputs may be any that keep to these rules, and one draw needn't show every extreme that they name: `sample_rows`: sample m indexes a row of box m // 6.
All inputs are finite; a program needn't handle non-finite values.
Results may differ from a plain program's by a relative error of at most 0.019.
Values may be sent and summed in bfloat16 or wider, within the bound.
A program may use at most 128 MiB of HBM per device.

v0:
```python
import jax
import jax.numpy as jnp
from jax import lax
from jax.sharding import PartitionSpec as P


def from_partner(array, axis, bit):
    return lax.ppermute(array, axis, [(i, i ^ 1 << bit) for i in range(lax.axis_size(axis))])


def per_device(vectors, leaf_in, leaf_out, factors, dense_rows, sample_rows):
    coefficients = jnp.dot(leaf_in, vectors, preferred_element_type=jnp.float32).astype(
        jnp.bfloat16
    )
    local_bits = lax.axis_size("lvl").bit_length() - 1
    group_bits = lax.axis_size("grp").bit_length() - 1
    own_factors = factors[0]

    def combine(step_index, current, opposite):
        mixed = jnp.dot(own_factors[step_index, 0], current, preferred_element_type=jnp.float32)
        mixed = mixed + jnp.dot(
            own_factors[step_index, 1], opposite, preferred_element_type=jnp.float32
        )
        return mixed.astype(jnp.bfloat16)

    for bit_index in range(local_bits):
        partner = from_partner(coefficients, "lvl", bit_index)
        coefficients = combine(bit_index, coefficients, partner)
    for bit_index in range(group_bits):
        partner = from_partner(coefficients, "grp", bit_index)
        coefficients = combine(local_bits + bit_index, coefficients, partner)
    picked = leaf_out[sample_rows]
    estimate = jnp.dot(picked, coefficients, preferred_element_type=jnp.float32)
    summed = lax.psum_scatter(
        jnp.dot(dense_rows, vectors, preferred_element_type=jnp.float32),
        ("grp", "lvl"),
        scatter_dimension=0,
        tiled=True,
    )
    return estimate - summed


def solution(mesh):
    return jax.shard_map(
        per_device,
        mesh=mesh,
        in_specs=(
            P(("grp", "lvl"), None),
            P(None, ("grp", "lvl")),
            P(("grp", "lvl"), None),
            P(("grp", "lvl"), None, None, None, None),
            P(None, ("grp", "lvl")),
            P(("grp", "lvl")),
        ),
        out_specs=P(("grp", "lvl"), None),
        check_vma=False,
    )
```

profile of v0, /device:TPU:8, one launch (start us, length us, event | category | flops | bytes accessed | tf_op | source)
XLA Modules:
  0.0 294.9 jit_solution(2658856726012193352)
XLA Ops:
  6.5 1.4 copy-done
  7.9 1.9 convolution_convert_fusion
  10.0 7.6 %fusion.18 = f32[1536,384]{1,0:T(8,128)} fusion(bf16[1536,2048]{1,0:T(8,128)(2,1)} %param.10, bf16[2048,384]{1,0:T(8,128)(2,1)S(1)} %copy-done), kind=kOutput, calls=%fused_computation.46 | convolution fusion | flops 2415919104 | bytes 10223616 | tf_op jit(solution)/shard_map/dot_general | solution.py:35
  18.3 1.9 gather_fusion
  20.2 1.2 fusion.17
  21.4 1.2 fusion
  22.6 2.3 collective-permute-start.1
  26.0 4.4 %collective-permute-done.1 = bf16[256,384]{0,1:T(8,128)(2,1)S(1)} collective-permute-done((bf16[256,384]{0,1:T(8,128)(2,1)S(1)}, bf16[256,384]{0,1:T(8,128)(2,1)S(1)}, u32[]{:S(2)}, u32[]{:S(2)}) %collective-permute-start.1) | collective-permute-done | bytes 196640 | tf_op jit(solution)/shard_map/ppermute | solution.py:8
  31.5 1.9 collective-permute-start.2
  34.6 5.4 %collective-permute-done.2 = bf16[256,384]{0,1:T(8,128)(2,1)S(1)} collective-permute-done((bf16[256,384]{0,1:T(8,128)(2,1)S(1)}, bf16[256,384]{0,1:T(8,128)(2,1)S(1)}, u32[]{:S(2)}, u32[]{:S(2)}) %collective-permute-start.2) | collective-permute-done | bytes 196640 | tf_op jit(solution)/shard_map/ppermute | solution.py:8
  40.0 1.2 fusion.2
  43.1 4.3 %collective-permute-done.3 = bf16[256,384]{0,1:T(8,128)(2,1)S(1)} collective-permute-done((bf16[256,384]{0,1:T(8,128)(2,1)S(1)}, bf16[256,384]{0,1:T(8,128)(2,1)S(1)}, u32[]{:S(2)}, u32[]{:S(2)}) %collective-permute-start.3) | collective-permute-done | bytes 196640 | tf_op jit(solution)/shard_map/ppermute | solution.py:8
  47.5 1.1 fusion.3
  48.6 2.2 collective-permute-start.4
  52.0 3.9 %collective-permute-done.4 = bf16[256,384]{0,1:T(8,128)(2,1)S(1)} collective-permute-done((bf16[256,384]{0,1:T(8,128)(2,1)S(1)}, bf16[256,384]{0,1:T(8,128)(2,1)S(1)}, u32[]{:S(2)}, u32[]{:S(2)}) %collective-permute-start.4) | collective-permute-done | bytes 196640 | tf_op jit(solution)/shard_map/ppermute | solution.py:8
  57.0 1.2 collective-permute-start.5
  59.4 3.7 %collective-permute-done.5 = bf16[256,384]{0,1:T(8,128)(2,1)S(1)} collective-permute-done((bf16[256,384]{0,1:T(8,128)(2,1)S(1)}, bf16[256,384]{0,1:T(8,128)(2,1)S(1)}, u32[]{:S(2)}, u32[]{:S(2)}) %collective-permute-start.5) | collective-permute-done | bytes 196640 | tf_op jit(solution)/shard_map/ppermute | solution.py:8
  63.1 1.1 fusion.5
  64.2 2.5 collective-permute-start.6
  67.8 5.7 %collective-permute-done.6 = bf16[256,384]{0,1:T(8,128)(2,1)S(1)} collective-permute-done((bf16[256,384]{0,1:T(8,128)(2,1)S(1)}, bf16[256,384]{0,1:T(8,128)(2,1)S(1)}, u32[]{:S(2)}, u32[]{:S(2)}) %collective-permute-start.6) | collective-permute-done | bytes 196640 | tf_op jit(solution)/shard_map/ppermute | solution.py:8
  73.6 1.1 fusion.6
  74.7 11.1 %collective-permute-start.7 = (bf16[256,384]{0,1:T(8,128)(2,1)S(1)}, bf16[256,384]{0,1:T(8,128)(2,1)S(1)}, u32[]{:S(2)}, u32[]{:S(2)}) collective-permute-start(bf16[256,384]{0,1:T(8,128)(2,1)S(1)} %bitcast.94), channel_id=1, source_target_pairs={{0,128},{32,160},{64,192},{96,224},{128,0},{160,32},{192,64},{224,... | collective-permute-start | bytes 589832 | tf_op jit(solution)/shard_map/ppermute | solution.py:8
  86.9 199.2 %all-reduce.3.cloned.1.call-done = f32[1536,384]{1,0:T(8,128)} async-done(((f32[1536,384]{1,0:T(8,128)}), f32[1536,384]{1,0:T(8,128)}) %all-reduce.3.cloned.1.call-update) | async-done | bytes 2359312
  286.1 1.9 fusion.9
  (20 shorter events, 11.9 us)
Async XLA Ops:
  6.5 1.4 copy-start
  6.5 279.6 %all-reduce.3.cloned.1.call-start = ((), (), s32[]{:S(2)}) async-start(), calls=%async_computation | async-start | bytes 4718592
  9.9 11.5 %collective-permute-start = (bf16[256,384]{1,0:T(8,128)(2,1)S(1)}, bf16[256,384]{1,0:T(8,128)(2,1)S(1)}, u32[]{:S(2)}, u32[]{:S(2)}) collective-permute-start(bf16[256,384]{1,0:T(8,128)(2,1)S(1)} %convolution_convert_fusion), channel_id=1, source_target_pairs={{0,1},{1,0},{2,3},{3,2},{4,5},{5,4},{6,7},{7,6},{8,9},{9,8},{10,11... | collective-permute-start | bytes 589832 | tf_op jit(solution)/shard_map/ppermute | solution.py:8
  17.6 0.7 copy-start.1
  22.6 7.8 %collective-permute-start.1 = (bf16[256,384]{0,1:T(8,128)(2,1)S(1)}, bf16[256,384]{0,1:T(8,128)(2,1)S(1)}, u32[]{:S(2)}, u32[]{:S(2)}) collective-permute-start(bf16[256,384]{0,1:T(8,128)(2,1)S(1)} %bitcast.95), channel_id=1, source_target_pairs={{0,2},{1,3},{2,0},{3,1},{4,6},{5,7},{6,4},{7,5},{8,10},{9,11},{10,... | collective-permute-start | bytes 589832 | tf_op jit(solution)/shard_map/ppermute | solution.py:8
  31.5 8.5 %collective-permute-start.2 = (bf16[256,384]{0,1:T(8,128)(2,1)S(1)}, bf16[256,384]{0,1:T(8,128)(2,1)S(1)}, u32[]{:S(2)}, u32[]{:S(2)}) collective-permute-start(bf16[256,384]{0,1:T(8,128)(2,1)S(1)} %bitcast.96), channel_id=1, source_target_pairs={{0,4},{1,5},{2,6},{3,7},{4,0},{5,1},{6,2},{7,3},{8,12},{9,13},{10,... | collective-permute-start | bytes 589832 | tf_op jit(solution)/shard_map/ppermute | solution.py:8
  41.1 6.3 %collective-permute-start.3 = (bf16[256,384]{0,1:T(8,128)(2,1)S(1)}, bf16[256,384]{0,1:T(8,128)(2,1)S(1)}, u32[]{:S(2)}, u32[]{:S(2)}) collective-permute-start(bf16[256,384]{0,1:T(8,128)(2,1)S(1)} %bitcast.97), channel_id=1, source_target_pairs={{0,8},{1,9},{2,10},{3,11},{4,12},{5,13},{6,14},{7,15},{8,0},{9,1},... | collective-permute-start | bytes 589832 | tf_op jit(solution)/shard_map/ppermute | solution.py:8
  48.6 7.3 %collective-permute-start.4 = (bf16[256,384]{0,1:T(8,128)(2,1)S(1)}, bf16[256,384]{0,1:T(8,128)(2,1)S(1)}, u32[]{:S(2)}, u32[]{:S(2)}) collective-permute-start(bf16[256,384]{0,1:T(8,128)(2,1)S(1)} %bitcast.98), channel_id=1, source_target_pairs={{0,16},{1,17},{2,18},{3,19},{4,20},{5,21},{6,22},{7,23},{8,24},{9,... | collective-permute-start | bytes 589832 | tf_op jit(solution)/shard_map/ppermute | solution.py:8
  57.0 6.1 %collective-permute-start.5 = (bf16[256,384]{0,1:T(8,128)(2,1)S(1)}, bf16[256,384]{0,1:T(8,128)(2,1)S(1)}, u32[]{:S(2)}, u32[]{:S(2)}) collective-permute-start(bf16[256,384]{0,1:T(8,128)(2,1)S(1)} %bitcast.99), channel_id=1, source_target_pairs={{0,32},{32,0},{64,96},{96,64},{128,160},{160,128},{192,224},{224,1... | collective-permute-start | bytes 589832 | tf_op jit(solution)/shard_map/ppermute | solution.py:8
  64.2 9.4 %collective-permute-start.6 = (bf16[256,384]{0,1:T(8,128)(2,1)S(1)}, bf16[256,384]{0,1:T(8,128)(2,1)S(1)}, u32[]{:S(2)}, u32[]{:S(2)}) collective-permute-start(bf16[256,384]{0,1:T(8,128)(2,1)S(1)} %bitcast.100), channel_id=1, source_target_pairs={{0,64},{32,96},{64,0},{96,32},{128,192},{160,224},{192,128},{224,1... | collective-permute-start | bytes 589832 | tf_op jit(solution)/shard_map/ppermute | solution.py:8
  74.7 211.4 %collective-permute-start.7 = (bf16[256,384]{0,1:T(8,128)(2,1)S(1)}, bf16[256,384]{0,1:T(8,128)(2,1)S(1)}, u32[]{:S(2)}, u32[]{:S(2)}) collective-permute-start(bf16[256,384]{0,1:T(8,128)(2,1)S(1)} %bitcast.94), channel_id=1, source_target_pairs={{0,128},{32,160},{64,192},{96,224},{128,0},{160,32},{192,64},{224,... | collective-permute-start | bytes 589832 | tf_op jit(solution)/shard_map/ppermute | solution.py:8
Sparse Core Ops, SparseCore 0:
  17.8 268.3 all-reduce.2
where the time goes:
time: 296 us; the launch traced here: 295 us
  waiting for transfers between devices  227 us (77%)
  matrix products  28.7 us (10%)
  starting transfers between devices  22.1 us (7%)
  between operations  13.5 us (5%)
  local copies, waits for them, and re-layouts  3.95 us (1%)
    unnamed x2, waiting for transfers between devices  199 us
    ppermute x8, waiting for transfers between devices, from_partner(): lax.ppermute(array, axis, [(i, i ^ 1 << bit) for i in range(lax.axis_size...  27.4 us
    ppermute x8, starting transfers between devices, from_partner(): lax.ppermute(array, axis, [(i, i ^ 1 << bit) for i in range(lax.axis_size...  22.1 us
    dot_general x8, matrix products, combine(): jnp.dot(own_factors[step_index, 0], current, preferred_element_type=jnp.f...  9.14 us
    dot_general x7, matrix products, combine(): jnp.dot(own_factors[step_index, 1], opposite, preferred_element_type=jnp....  8.05 us
    dot_general x1, matrix products, per_device(): jnp.dot(dense_rows, vectors, preferred_element_type=jnp.float32)  7.63 us
  transfers between devices with their start and end apart: 9, of which 7 were waited for; matrix products, arithmetic and copies ran while one was open for 9% of the time, Pallas kernels for 0%

commit v1 on v0

v1 whole, which is shorter than its diff:
```python
import functools

import jax
import jax.numpy as jnp
from jax import lax
from jax.experimental import pallas as pl
from jax.experimental.pallas import tpu as pltpu
from jax.sharding import PartitionSpec as P

MESH = pl.DeviceIdType.MESH
BF16, F32 = jnp.bfloat16, jnp.float32

ROWS, RANK, VECS, SAMP = 2048, 256, 384, 6
Z, X, Y = 8, 4, 4
BLOCK = Z * SAMP
HALF = Y * BLOCK
CHUNK = 128
CHUNKS = VECS // CHUNK
PAD = 16
GROUPS = (0, 4, 2, 6, 1, 5, 3, 7)


def dot(a, b):
    return jnp.dot(a, b, preferred_element_type=F32)


def dot16(a, b):
    return dot(a, b).astype(BF16)


def count_steps(values, step, steps):
    total = jnp.zeros_like(values)
    for i in range(1, steps):
        total = total + (values >= i * step).astype(jnp.int32)
    return total


def permutation(core, y):
    row = lax.broadcasted_iota(jnp.int32, (2 * HALF, 1), 0)
    half = count_steps(row, HALF, 2)
    row = row - half * HALF
    quarter = count_steps(row, BLOCK, Y)
    row = row - quarter * BLOCK
    z = count_steps(row, SAMP, Z)
    sample = row - z * SAMP
    source = z * BLOCK + (quarter ^ y) * (2 * SAMP) + (half ^ core) * SAMP + sample
    column = lax.broadcasted_iota(jnp.int32, (2 * HALF, 2 * HALF), 1)
    return jnp.where(column == source, 1.0, 0.0).astype(BF16)


def spread(z):
    row = lax.broadcasted_iota(jnp.int32, (Z * PAD, 1), 0)
    group = count_steps(row, PAD, Z)
    sample = row - group * PAD
    offset = jnp.zeros_like(group)
    for i, value in enumerate(GROUPS):
        offset = offset + jnp.where(group == i, value, 0)
    source = jnp.where(sample < SAMP, (offset ^ z) * SAMP + sample, -1)
    column = lax.broadcasted_iota(jnp.int32, (Z * PAD, BLOCK), 1)
    return jnp.where(column == source, 1.0, 0.0).astype(BF16)


def kernel(
    samp, vec_hbm, lin_hbm, lout_hbm, fac_hbm, dense_hbm, out,
    vec, lin, lout, fac, dense, perm,
    c0_send, c0_recv, far_y, far_x, c1, y_recv, c3, x_recv,
    half_send, half_recv, mine, xs_send, xs_recv, ys_send, ys_recv, total_y,
    w_send4, w_recv4, w_send2, w_recv2, w_send1, w_recv1, w_all, exact,
    tail_send, tail_recv, local_sem, send_sem, recv_sem,
):
    z, lvl = lax.axis_index("grp"), lax.axis_index("lvl")
    x, y, core = lvl // 8, (lvl // 2) % 4, lvl % 2

    def core_peer():
        return (z, lvl ^ 1)

    def y_peer(j):
        return (z, lvl ^ (2 * j))

    def x_peer(j):
        return (z, lvl ^ (8 * j))

    def z_peer(j):
        return (z ^ j, lvl)

    peers = [core_peer()] + [y_peer(j) for j in (1, 2, 3)] + [x_peer(j) for j in (1, 2, 3)]
    peers += [z_peer(j) for j in range(1, Z)]
    barrier = pltpu.get_barrier_semaphore()
    for peer in peers:
        pl.semaphore_signal(barrier, inc=1, device_id=peer, device_id_type=MESH)

    used = [0, 0]
    sent = []

    def load(source, target):
        copy = pltpu.make_async_copy(source, target, local_sem.at[used[0]])
        used[0] += 1
        copy.start()
        return copy

    def send(source, target, peer):
        copy = pltpu.make_async_remote_copy(
            src_ref=source,
            dst_ref=target,
            send_sem=send_sem.at[used[1]],
            recv_sem=recv_sem.at[used[1]],
            device_id=peer,
            device_id_type=MESH,
        )
        used[1] += 1
        copy.start()
        sent.append(copy)
        return copy

    def load_factors(level):
        return load(fac_hbm.at[0, level], fac.at[level])

    def load_dense(j):
        copies = []
        for group in range(Z):
            first = pl.multiple_of(group * (X * BLOCK) + (x ^ j) * BLOCK, BLOCK)
            copies.append(
                load(dense_hbm.at[pl.ds(first, BLOCK), :], dense.at[j, pl.ds(group * BLOCK, BLOCK), :])
            )
        return copies

    got_lout = load(lout_hbm, lout)
    got_fac = {7: load_factors(7)}
    got_lin, got_vec = load(lin_hbm, lin), load(vec_hbm, vec)
    got_fac[0] = load_factors(0)
    got_dense = {}
    order = (1, 2, 3, 0)
    for j in order[:2]:
        got_dense[j] = load_dense(j)
    got_fac[6] = load_factors(6)
    for j in order[2:]:
        got_dense[j] = load_dense(j)
    for level in (1, 2, 5, 3, 4):
        got_fac[level] = load_factors(level)

    column = lax.broadcasted_iota(jnp.int32, (PAD, ROWS), 1)
    row = lax.broadcasted_iota(jnp.int32, (PAD, ROWS), 0)
    hot = jnp.zeros((PAD, ROWS), F32)
    for i in range(SAMP):
        hot = jnp.where((row == i) & (column == samp[i]), 1.0, hot)
    hot = hot.astype(BF16)
    got_lout.wait()
    w = dot16(hot, lout[...])
    got_fac[7].wait()
    w_send4[...] = dot16(w, fac[7, 1])
    own4 = dot16(w, fac[7, 0])

    perm[...] = permutation(core, y)

    got_lin.wait()
    got_vec.wait()
    c0_send[...] = dot16(lin[...], vec[...])

    pl.semaphore_wait(barrier, len(peers))
    move4 = send(w_send4, w_recv4, z_peer(4))
    move_c0 = send(c0_send, c0_recv, core_peer())
    move_far_y = send(fac_hbm.at[0, 1], far_y, y_peer(2))
    move_far_x = send(fac_hbm.at[0, 3], far_x, x_peer(2))

    def dense_product(j):
        for copy in got_dense[j]:
            copy.wait()
        product = dot16(dense[j], vec[...])
        product = dot(perm[...], product)
        mine[j] = product[:HALF]
        half_send[j] = product[HALF:].astype(BF16)
        return send(half_send.at[j], half_recv.at[j], core_peer())

    move_half = {}
    for j in (1, 2):
        move_half[j] = dense_product(j)

    got_fac[0].wait()
    move_c0.wait_recv()
    c1[...] = (dot(fac[0, 0], c0_send[...]) + dot(fac[0, 1], c0_recv[...])).astype(BF16)
    move_c1 = {}
    for k in range(CHUNKS):
        columns = pl.ds(k * CHUNK, CHUNK)
        for j in (2, 1, 3):
            move_c1[k, j] = send(c1.at[:, columns], y_recv.at[j - 1, :, columns], y_peer(j))

    for j in (3, 0):
        move_half[j] = dense_product(j)

    move_xs = {}
    for j in (1, 2, 3):
        move_half[j].wait_recv()
        xs_send[j - 1] = (mine[j] + half_recv[j].astype(F32)).astype(BF16)
        move_xs[j] = send(xs_send.at[j - 1], xs_recv.at[j - 1], x_peer(j))

    got_fac[6].wait()
    move4.wait_recv()
    w = jnp.concatenate([own4, w_recv4[...]], axis=0)
    w_send2[...] = dot16(w, fac[6, 1])
    move2 = send(w_send2, w_recv2, z_peer(2))
    own2 = dot16(w, fac[6, 0])

    def combine(level, far, near, others, columns):
        a = (dot(fac[level, 0], near) + dot(fac[level, 1], others[0, :, columns])).astype(BF16)
        b = (dot(far[0], others[1, :, columns]) + dot(far[1], others[2, :, columns])).astype(BF16)
        return (dot(fac[level + 1, 0], a) + dot(fac[level + 1, 1], b)).astype(BF16)

    for level in (1, 2, 5, 3, 4):
        got_fac[level].wait()
    move_far_y.wait_recv()
    move_c3 = {}

    def y_levels(k):
        columns = pl.ds(k * CHUNK, CHUNK)
        for j in (1, 2, 3):
            move_c1[k, j].wait_recv()
        c3[:, columns] = combine(1, far_y, c1[:, columns], y_recv, columns)
        for j in (2, 1, 3):
            move_c3[k, j] = send(c3.at[:, columns], x_recv.at[j - 1, :, columns], x_peer(j))

    y_levels(0)

    move2.wait_recv()
    w = jnp.concatenate([own2, w_recv2[...]], axis=0)
    w_send1[...] = dot16(w, fac[5, 1])
    move1 = send(w_send1, w_recv1, z_peer(1))
    w_all[: 4 * PAD] = dot16(w, fac[5, 0])

    y_levels(1)

    move_half[0].wait_recv()
    total = mine[0] + half_recv[0].astype(F32)
    for j in (1, 2, 3):
        move_xs[j].wait_recv()
        total = total + xs_recv[j - 1].astype(F32)
    total_y[...] = total[:BLOCK]
    move_ys = {}
    for j in (1, 2, 3):
        ys_send[j - 1] = total[j * BLOCK : (j + 1) * BLOCK].astype(BF16)
        move_ys[j] = send(ys_send.at[j - 1], ys_recv.at[j - 1], y_peer(j))

    y_levels(2)

    total = total_y[...]
    for j in (1, 2, 3):
        move_ys[j].wait_recv()
        total = total + ys_recv[j - 1].astype(F32)
    high = total.astype(BF16)
    low = (total - high.astype(F32)).astype(BF16)
    onto = spread(z)
    exact[...] = dot(onto, high) + dot(onto, low)

    move1.wait_recv()
    w_all[4 * PAD :] = w_recv1[...]
    move_far_x.wait_recv()

    move_tail = {}
    for k in range(CHUNKS):
        columns = pl.ds(k * CHUNK, CHUNK)
        for j in (1, 2, 3):
            move_c3[k, j].wait_recv()
        c5 = combine(3, far_x, c3[:, columns], x_recv, columns)
        part = dot(w_all[...], c5) - exact[:, columns]
        for i in range(Z):
            tail_send[k, i] = part[i * PAD : i * PAD + 8]
        for i in range(1, Z):
            move_tail[k, i] = send(tail_send.at[k, i], tail_recv.at[k, i], z_peer(GROUPS[i]))

    for k in range(CHUNKS):
        part = tail_send[k, 0]
        for i in range(1, Z):
            move_tail[k, i].wait_recv()
            part = part + tail_recv[k, i]
        out[:, pl.ds(k * CHUNK, CHUNK)] = part[:SAMP]
    for copy in sent:
        copy.wait_send()


LOCAL = 4 + 7 + Z * X
REMOTE = 4 + 4 + 2 * 3 * CHUNKS + 6 + 2 + (Z - 1) * CHUNKS


def per_device(vectors, leaf_in, leaf_out, factors, dense_rows, sample_rows):
    vmem = pltpu.VMEM
    scratch = [
        vmem((ROWS, VECS), BF16),
        vmem((RANK, ROWS), BF16),
        vmem((ROWS, RANK), BF16),
        vmem((8, 2, RANK, RANK), BF16),
        vmem((X, 2 * HALF, ROWS), BF16),
        vmem((2 * HALF, 2 * HALF), BF16),
        vmem((RANK, VECS), BF16),
        vmem((RANK, VECS), BF16),
        vmem((2, RANK, RANK), BF16),
        vmem((2, RANK, RANK), BF16),
        vmem((RANK, VECS), BF16),
        vmem((3, RANK, VECS), BF16),
        vmem((RANK, VECS), BF16),
        vmem((3, RANK, VECS), BF16),
        vmem((X, HALF, VECS), BF16),
        vmem((X, HALF, VECS), BF16),
        vmem((X, HALF, VECS), F32),
        vmem((3, HALF, VECS), BF16),
        vmem((3, HALF, VECS), BF16),
        vmem((3, BLOCK, VECS), BF16),
        vmem((3, BLOCK, VECS), BF16),
        vmem((BLOCK, VECS), F32),
        vmem((PAD, RANK), BF16),
        vmem((PAD, RANK), BF16),
        vmem((2 * PAD, RANK), BF16),
        vmem((2 * PAD, RANK), BF16),
        vmem((4 * PAD, RANK), BF16),
        vmem((4 * PAD, RANK), BF16),
        vmem((8 * PAD, RANK), BF16),
        vmem((8 * PAD, VECS), F32),
        vmem((CHUNKS, Z, 8, CHUNK), F32),
        vmem((CHUNKS, Z, 8, CHUNK), F32),
        pltpu.SemaphoreType.DMA((LOCAL,)),
        pltpu.SemaphoreType.DMA((REMOTE,)),
        pltpu.SemaphoreType.DMA((REMOTE,)),
    ]
    anywhere = pl.BlockSpec(memory_space=pl.ANY)
    return pl.pallas_call(
        kernel,
        out_shape=jax.ShapeDtypeStruct((SAMP, VECS), F32),
        in_specs=[pl.BlockSpec(memory_space=pltpu.SMEM)] + [anywhere] * 5,
        out_specs=pl.BlockSpec(memory_space=pltpu.VMEM),
        scratch_shapes=scratch,
        compiler_params=pltpu.CompilerParams(
            collective_id=0, has_side_effects=True, vmem_limit_bytes=56 * 2**20
        ),
        cost_estimate=pl.CostEstimate(
            flops=2 * 1700 * 10**6, bytes_accessed=12 * 2**20, transcendentals=0
        ),
    )(sample_rows, vectors, leaf_in, leaf_out, factors, dense_rows)


def solution(mesh):
    return jax.shard_map(
        per_device,
        mesh=mesh,
        in_specs=(
            P(("grp", "lvl"), None),
            P(None, ("grp", "lvl")),
            P(("grp", "lvl"), None),
            P(("grp", "lvl"), None, None, None, None),
            P(None, ("grp", "lvl")),
            P(("grp", "lvl")),
        ),
        out_specs=P(("grp", "lvl"), None),
        check_vma=False,
    )
```

time: 296 us -> 42.4 us (0.14)
  the two profiles are of different devices: /device:TPU:8 before, /device:TPU:1 now
where the time goes in v1:
time: 42.4 us; the launch traced here: 42.2 us
  Pallas kernels  40.9 us (96%)
  local copies, waits for them, and re-layouts  1.31 us (3%)
    pallas_call x1, Pallas kernels, per_device(): pl.pallas_call(kernel, out_shape=jax.ShapeDtypeStruct((SAMP, VECS), F32),...  40.9 us
    unnamed x1, local copies, waits for them, and re-layouts  1.31 us

profile of v1, /device:TPU:1, one launch (start us, length us, event | category | flops | bytes accessed | tf_op | source)
XLA Modules:
  0.0 42.2 jit_solution(7699779048255002160)
XLA Ops:
  0.0 40.9 %shard_map.64 = f32[6,384]{1,0:T(8,128)} custom-call(s32[6]{0:T(128)} %samp.1, bf16[2048,384]{1,0:T(8,128)(2,1)} %vec_hbm.1, bf16[256,2048]{1,0:T(8,128)(2,1)} %lin_hbm.1, bf16[2048,256]{1,0:T(8,128)(2,1)} %lout_hbm.1, bf16[1,8,2,256,256]{4,3,2,1,0:T(8,128)(2,1)} %fac_hbm.1, bf16[1536,2048]{1,0:T(8,128)(2,1)} %dense_hbm.1), custom_call_target="tpu_custom_call" | custom-call | flops 3400000000 | bytes 12582912 | tf_op jit(solution)/shard_map/pallas_call | solution.py:323
  40.9 1.3 %copy.8 = f32[6,384]{1,0:T(8,128)} copy(f32[6,384]{1,0:T(8,128)} %shard_map.64) | data formatting | bytes 18432

commit v2 on v1

v2 whole, which is shorter than its diff:
```python
import functools

import jax
import jax.numpy as jnp
from jax import lax
from jax.experimental import pallas as pl
from jax.experimental.pallas import tpu as pltpu
from jax.sharding import PartitionSpec as P

MESH = pl.DeviceIdType.MESH
BF16, F32 = jnp.bfloat16, jnp.float32

ROWS, RANK, VECS, SAMP = 2048, 256, 384, 6
Z, X, Y = 8, 4, 4
BLOCK = Z * SAMP
HALF = Y * BLOCK
CHUNK = 128
CHUNKS = VECS // CHUNK
ROOM = 8
GROUPS = (0, 4, 2, 6, 1, 5, 3, 7)


def dot(a, b):
    return jnp.dot(a, b, preferred_element_type=F32)


def dot16(a, b):
    return dot(a, b).astype(BF16)


def count_steps(values, step, steps):
    total = jnp.zeros_like(values)
    for i in range(1, steps):
        total = total + (values >= i * step).astype(jnp.int32)
    return total


def permutation(core, y):
    row = lax.broadcasted_iota(jnp.int32, (2 * HALF, 1), 0)
    half = count_steps(row, HALF, 2)
    row = row - half * HALF
    quarter = count_steps(row, BLOCK, Y)
    row = row - quarter * BLOCK
    z = count_steps(row, SAMP, Z)
    sample = row - z * SAMP
    source = z * BLOCK + (quarter ^ y) * (2 * SAMP) + (half ^ core) * SAMP + sample
    column = lax.broadcasted_iota(jnp.int32, (2 * HALF, 2 * HALF), 1)
    return jnp.where(column == source, 1.0, 0.0).astype(BF16)


def spread(z):
    row = lax.broadcasted_iota(jnp.int32, (Z * ROOM, 1), 0)
    group = count_steps(row, ROOM, Z)
    sample = row - group * ROOM
    offset = jnp.zeros_like(group)
    for i, value in enumerate(GROUPS):
        offset = offset + jnp.where(group == i, value, 0)
    source = jnp.where(sample < SAMP, (offset ^ z) * SAMP + sample, -1)
    column = lax.broadcasted_iota(jnp.int32, (Z * ROOM, BLOCK), 1)
    return jnp.where(column == source, 1.0, 0.0).astype(BF16)


def kernel(
    samp, vec_hbm, lin_hbm, lout_hbm, fac_hbm, dense_hbm, out,
    vec, lin, lout, fac, dense, perm,
    c0_send, c0_recv, c1, c1_recv, c2, c2_recv, c3, c3_recv,
    half_send, half_recv, mine, xs_send, xs_recv, ys_send, ys_recv, total_y,
    w_send4, w_recv4, w_send2, w_recv2, w_send1, w_recv1, w_send_x, w_recv_x, w_all,
    tail_send, tail_recv, local_sem, send_sem, recv_sem,
):
    z, lvl = lax.axis_index("grp"), lax.axis_index("lvl")
    x, y, core = lvl // 8, (lvl // 2) % 4, lvl % 2

    def core_peer():
        return (z, lvl ^ 1)

    def y_peer(j):
        return (z, lvl ^ (2 * j))

    def x_peer(j):
        return (z, lvl ^ (8 * j))

    def z_peer(j):
        return (z ^ j, lvl)

    def tail_peer(i):
        return (z ^ GROUPS[i % Z], lvl ^ (16 * (i // Z)))

    peers = [core_peer()] + [y_peer(j) for j in (1, 2, 3)] + [x_peer(j) for j in (1, 3)]
    peers += [tail_peer(i) for i in range(1, 2 * Z)]
    barrier = pltpu.get_barrier_semaphore()
    for peer in peers:
        pl.semaphore_signal(barrier, inc=1, device_id=peer, device_id_type=MESH)

    used = [0, 0]
    sent = []

    def load(source, target):
        copy = pltpu.make_async_copy(source, target, local_sem.at[used[0]])
        used[0] += 1
        copy.start()
        return copy

    def send(source, target, peer):
        copy = pltpu.make_async_remote_copy(
            src_ref=source,
            dst_ref=target,
            send_sem=send_sem.at[used[1]],
            recv_sem=recv_sem.at[used[1]],
            device_id=peer,
            device_id_type=MESH,
        )
        used[1] += 1
        copy.start()
        sent.append(copy)
        return copy

    def load_factors(level):
        return load(fac_hbm.at[0, level], fac.at[level])

    def load_dense(j):
        copies = []
        for group in range(Z):
            first = pl.multiple_of(group * (X * BLOCK) + (x ^ j) * BLOCK, BLOCK)
            copies.append(
                load(dense_hbm.at[pl.ds(first, BLOCK), :], dense.at[j, pl.ds(group * BLOCK, BLOCK), :])
            )
        return copies

    got_lin, got_vec = load(lin_hbm, lin), load(vec_hbm, vec)
    got_lout = load(lout_hbm, lout)
    got_fac = {7: load_factors(7)}
    got_fac[0] = load_factors(0)
    got_dense = {}
    order = (2, 1, 3, 0)
    for j in order[:2]:
        got_dense[j] = load_dense(j)
    got_fac[1] = load_factors(1)
    got_fac[6] = load_factors(6)
    for j in order[2:]:
        got_dense[j] = load_dense(j)
    for level in (2, 5, 3, 4):
        got_fac[level] = load_factors(level)

    column = lax.broadcasted_iota(jnp.int32, (2 * ROOM, ROWS), 1)
    row = lax.broadcasted_iota(jnp.int32, (2 * ROOM, ROWS), 0)
    hot = jnp.zeros((2 * ROOM, ROWS), F32)
    for i in range(SAMP):
        hot = jnp.where((row == i) & (column == samp[i]), 1.0, hot)
    hot = hot.astype(BF16)
    perm[...] = permutation(core, y)

    got_lin.wait()
    got_vec.wait()
    c0_send[...] = dot16(lin[...], vec[...])

    got_lout.wait()
    w = dot16(hot, lout[...])
    got_fac[7].wait()
    w_send4[...] = dot16(w, fac[7, 1])
    own4 = dot(w, fac[7, 0])[:ROOM]

    pl.semaphore_wait(barrier, len(peers))
    move4 = send(w_send4, w_recv4, z_peer(4))
    move_c0 = send(c0_send, c0_recv, core_peer())

    def dense_product(j):
        for copy in got_dense[j]:
            copy.wait()
        product = dot16(dense[j], vec[...])
        product = dot(perm[...], product)
        mine[j] = product[:HALF]
        half_send[j] = product[HALF:].astype(BF16)
        return send(half_send.at[j], half_recv.at[j], core_peer())

    move_half = {2: dense_product(2)}
    got_fac[0].wait()
    near = dot(fac[0, 0], c0_send[...])
    move_c0.wait_recv()
    c1[...] = (near + dot(fac[0, 1], c0_recv[...])).astype(BF16)

    columns = [pl.ds(k * CHUNK, CHUNK) for k in range(CHUNKS)]

    def exchange(k, ref, landing, peer):
        return send(ref.at[:, columns[k]], landing.at[:, columns[k]], peer)

    def combine(level, k, ref, landing, move, result):
        near = dot(fac[level, 0], ref[:, columns[k]])
        move.wait_recv()
        far = dot(fac[level, 1], landing[:, columns[k]])
        result[:, columns[k]] = (near + far).astype(BF16)

    def send_half(j):
        move_half[j].wait_recv()
        xs_send[j - 1] = (mine[j] + half_recv[j].astype(F32)).astype(BF16)
        return send(xs_send.at[j - 1], xs_recv.at[j - 1], x_peer(j))

    move_c1 = [exchange(k, c1, c1_recv, y_peer(1)) for k in range(CHUNKS)]
    move_xs, move_c2, move_c3 = {}, {}, {}
    move_half[1] = dense_product(1)
    move_xs[2] = send_half(2)
    move_half[3] = dense_product(3)
    move_xs[1] = send_half(1)
    move_half[0] = dense_product(0)
    move_xs[3] = send_half(3)

    got_fac[6].wait()
    move4.wait_recv()
    w = jnp.concatenate([own4, w_recv4[...].astype(F32)[:ROOM]], axis=0).astype(BF16)
    w_send2[...] = dot16(w, fac[6, 1])
    move2 = send(w_send2, w_recv2, z_peer(2))
    own2 = dot16(w, fac[6, 0])

    got_fac[1].wait()
    for k in range(CHUNKS):
        combine(1, k, c1, c1_recv, move_c1[k], c2)
        move_c2[k] = exchange(k, c2, c2_recv, y_peer(2))

    got_fac[5].wait()
    move2.wait_recv()
    w = jnp.concatenate([own2, w_recv2[...]], axis=0)
    w_send1[...] = dot16(w, fac[5, 1])
    move1 = send(w_send1, w_recv1, z_peer(1))
    own1 = dot16(w, fac[5, 0])

    got_fac[2].wait()
    combine(2, 0, c2, c2_recv, move_c2[0], c3)
    move_c3[0] = exchange(0, c3, c3_recv, x_peer(1))

    got_fac[4].wait()
    move1.wait_recv()
    w = jnp.concatenate([own1, w_recv1[...]], axis=0)
    w_send_x[...] = dot16(w, fac[4, 1])
    move_x = send(w_send_x, w_recv_x, x_peer(2))
    w_all[: Z * ROOM] = dot16(w, fac[4, 0])

    combine(2, 1, c2, c2_recv, move_c2[1], c3)
    move_c3[1] = exchange(1, c3, c3_recv, x_peer(1))

    combine(2, 2, c2, c2_recv, move_c2[2], c3)
    move_c3[2] = exchange(2, c3, c3_recv, x_peer(1))

    move_half[0].wait_recv()
    total = mine[0] + half_recv[0].astype(F32)
    for j in (1, 2, 3):
        move_xs[j].wait_recv()
        total = total + xs_recv[j - 1].astype(F32)
    total_y[...] = total[:BLOCK]
    move_ys = {}
    for j in (1, 2, 3):
        ys_send[j - 1] = total[j * BLOCK : (j + 1) * BLOCK].astype(BF16)
        move_ys[j] = send(ys_send.at[j - 1], ys_recv.at[j - 1], y_peer(j))

    got_fac[3].wait()
    onto = spread(z)
    move_x.wait_recv()
    w_all[Z * ROOM :] = w_recv_x[...]
    w = w_all[...]

    move_tail = {}

    def send_tail(k, i):
        move_tail[k, i] = send(tail_send.at[k, i], tail_recv.at[k, i], tail_peer(i))

    for k in range(CHUNKS):
        near = dot(fac[3, 0], c3[:, columns[k]])
        move_c3[k].wait_recv()
        far = dot(fac[3, 1], c3_recv[:, columns[k]])
        part = dot(w, (near + far).astype(BF16))
        for i in range(2 * Z):
            tail_send[k, i] = part[i * ROOM : (i + 1) * ROOM]
        for i in range(Z, 2 * Z):
            send_tail(k, i)

    total = total_y[...]
    for j in (1, 2, 3):
        move_ys[j].wait_recv()
        total = total + ys_recv[j - 1].astype(F32)
    high = total.astype(BF16)
    low = (total - high.astype(F32)).astype(BF16)
    exact = dot(onto, high) + dot(onto, low)
    for i in range(Z):
        for k in range(CHUNKS):
            rows = exact[i * ROOM : (i + 1) * ROOM, k * CHUNK : (k + 1) * CHUNK]
            tail_send[k, i] = tail_send[k, i] - rows
            if i > 0:
                send_tail(k, i)

    for k in range(CHUNKS):
        part = tail_send[k, 0]
        for i in range(1, 2 * Z):
            move_tail[k, i].wait_recv()
            part = part + tail_recv[k, i]
        out[:, columns[k]] = part[:SAMP]
    for copy in sent:
        copy.wait_send()


LOCAL = 3 + 8 + Z * X
REMOTE = 1 + 3 * CHUNKS + 4 + 3 + 3 + 4 + (2 * Z - 1) * CHUNKS


def per_device(vectors, leaf_in, leaf_out, factors, dense_rows, sample_rows):
    vmem = pltpu.VMEM
    scratch = [
        vmem((ROWS, VECS), BF16),
        vmem((RANK, ROWS), BF16),
        vmem((ROWS, RANK), BF16),
        vmem((8, 2, RANK, RANK), BF16),
        vmem((X, 2 * HALF, ROWS), BF16),
        vmem((2 * HALF, 2 * HALF), BF16),
        vmem((RANK, VECS), BF16),
        vmem((RANK, VECS), BF16),
        vmem((RANK, VECS), BF16),
        vmem((RANK, VECS), BF16),
        vmem((RANK, VECS), BF16),
        vmem((RANK, VECS), BF16),
        vmem((RANK, VECS), BF16),
        vmem((RANK, VECS), BF16),
        vmem((X, HALF, VECS), BF16),
        vmem((X, HALF, VECS), BF16),
        vmem((X, HALF, VECS), F32),
        vmem((3, HALF, VECS), BF16),
        vmem((3, HALF, VECS), BF16),
        vmem((3, BLOCK, VECS), BF16),
        vmem((3, BLOCK, VECS), BF16),
        vmem((BLOCK, VECS), F32),
        vmem((2 * ROOM, RANK), BF16),
        vmem((2 * ROOM, RANK), BF16),
        vmem((2 * ROOM, RANK), BF16),
        vmem((2 * ROOM, RANK), BF16),
        vmem((4 * ROOM, RANK), BF16),
        vmem((4 * ROOM, RANK), BF16),
        vmem((8 * ROOM, RANK), BF16),
        vmem((8 * ROOM, RANK), BF16),
        vmem((16 * ROOM, RANK), BF16),
        vmem((CHUNKS, 2 * Z, ROOM, CHUNK), F32),
        vmem((CHUNKS, 2 * Z, ROOM, CHUNK), F32),
        pltpu.SemaphoreType.DMA((LOCAL,)),
        pltpu.SemaphoreType.DMA((REMOTE,)),
        pltpu.SemaphoreType.DMA((REMOTE,)),
    ]
    anywhere = pl.BlockSpec(memory_space=pl.ANY)
    return pl.pallas_call(
        kernel,
        out_shape=jax.ShapeDtypeStruct((SAMP, VECS), F32),
        in_specs=[pl.BlockSpec(memory_space=pltpu.SMEM)] + [anywhere] * 5,
        out_specs=pl.BlockSpec(memory_space=pltpu.VMEM),
        scratch_shapes=scratch,
        compiler_params=pltpu.CompilerParams(
            collective_id=0, has_side_effects=True, vmem_limit_bytes=56 * 2**20
        ),
        cost_estimate=pl.CostEstimate(
            flops=2 * 1700 * 10**6, bytes_accessed=12 * 2**20, transcendentals=0
        ),
    )(sample_rows, vectors, leaf_in, leaf_out, factors, dense_rows)


def solution(mesh):
    return jax.shard_map(
        per_device,
        mesh=mesh,
        in_specs=(
            P(("grp", "lvl"), None),
            P(None, ("grp", "lvl")),
            P(("grp", "lvl"), None),
            P(("grp", "lvl"), None, None, None, None),
            P(None, ("grp", "lvl")),
            P(("grp", "lvl")),
        ),
        out_specs=P(("grp", "lvl"), None),
        check_vma=False,
    )
```

time: 42.4 us -> 38.1 us (0.90)
  the two profiles are of different devices: /device:TPU:1 before, /device:TPU:8 now
where the time goes in v2:
time: 38.1 us; the launch traced here: 37.8 us
  Pallas kernels  36.5 us (96%)
  local copies, waits for them, and re-layouts  1.31 us (3%)
    pallas_call x1, Pallas kernels, per_device(): pl.pallas_call(kernel, out_shape=jax.ShapeDtypeStruct((SAMP, VECS), F32),...  36.5 us
    unnamed x1, local copies, waits for them, and re-layouts  1.31 us

profile of v2, /device:TPU:8, one launch (start us, length us, event | category | flops | bytes accessed | tf_op | source)
XLA Modules:
  0.0 37.8 jit_solution(11710160041686516860)
XLA Ops:
  0.0 36.5 %shard_map.64 = f32[6,384]{1,0:T(8,128)} custom-call(s32[6]{0:T(128)} %samp.1, bf16[2048,384]{1,0:T(8,128)(2,1)} %vec_hbm.1, bf16[256,2048]{1,0:T(8,128)(2,1)} %lin_hbm.1, bf16[2048,256]{1,0:T(8,128)(2,1)} %lout_hbm.1, bf16[1,8,2,256,256]{4,3,2,1,0:T(8,128)(2,1)} %fac_hbm.1, bf16[1536,2048]{1,0:T(8,128)(2,1)} %dense_hbm.1), custom_call_target="tpu_custom_call" | custom-call | flops 3400000000 | bytes 12582912 | tf_op jit(solution)/shard_map/pallas_call | solution.py:344
  36.5 1.3 %copy.8 = f32[6,384]{1,0:T(8,128)} copy(f32[6,384]{1,0:T(8,128)} %shard_map.64) | data formatting | bytes 18432

commit v3 on v2

--- a/solution.py
+++ b/solution.py
@@ -66,7 +66,7 @@
     c0_send, c0_recv, c1, c1_recv, c2, c2_recv, c3, c3_recv,
     half_send, half_recv, mine, xs_send, xs_recv, ys_send, ys_recv, total_y,
     w_send4, w_recv4, w_send2, w_recv2, w_send1, w_recv1, w_send_x, w_recv_x, w_all,
-    tail_send, tail_recv, local_sem, send_sem, recv_sem,
+    tail_send, tail_recv, last_send, last_recv, local_sem, send_sem, recv_sem,
 ):
     z, lvl = lax.axis_index("grp"), lax.axis_index("lvl")
     x, y, core = lvl // 8, (lvl // 2) % 4, lvl % 2
@@ -86,10 +86,10 @@
     def tail_peer(i):
         return (z ^ GROUPS[i % Z], lvl ^ (16 * (i // Z)))
 
-    peers = [core_peer()] + [y_peer(j) for j in (1, 2, 3)] + [x_peer(j) for j in (1, 3)]
-    peers += [tail_peer(i) for i in range(1, 2 * Z)]
+    peers = [core_peer()] + [y_peer(j) for j in (1, 2, 3)] + [x_peer(j) for j in (1, 2, 3)]
+    peers += [tail_peer(i) for i in range(1, Z)]
     barrier = pltpu.get_barrier_semaphore()
-    for peer in peers:
+    for peer in peers[::-1]:
         pl.semaphore_signal(barrier, inc=1, device_id=peer, device_id_type=MESH)
 
     used = [0, 0]
@@ -204,6 +204,10 @@
     move_half[0] = dense_product(0)
     move_xs[3] = send_half(3)
 
+    got_fac[1].wait()
+    combine(1, 0, c1, c1_recv, move_c1[0], c2)
+    move_c2[0] = exchange(0, c2, c2_recv, y_peer(2))
+
     got_fac[6].wait()
     move4.wait_recv()
     w = jnp.concatenate([own4, w_recv4[...].astype(F32)[:ROOM]], axis=0).astype(BF16)
@@ -211,8 +215,7 @@
     move2 = send(w_send2, w_recv2, z_peer(2))
     own2 = dot16(w, fac[6, 0])
 
-    got_fac[1].wait()
-    for k in range(CHUNKS):
+    for k in range(1, CHUNKS):
         combine(1, k, c1, c1_recv, move_c1[k], c2)
         move_c2[k] = exchange(k, c2, c2_recv, y_peer(2))
 
@@ -260,16 +263,16 @@
     move_tail = {}
 
     def send_tail(k, i):
-        move_tail[k, i] = send(tail_send.at[k, i], tail_recv.at[k, i], tail_peer(i))
+        move_tail[k, i] = send(tail_send.at[k, i], tail_recv.at[k, i], tail_peer(Z + i))
 
     for k in range(CHUNKS):
         near = dot(fac[3, 0], c3[:, columns[k]])
         move_c3[k].wait_recv()
         far = dot(fac[3, 1], c3_recv[:, columns[k]])
         part = dot(w, (near + far).astype(BF16))
-        for i in range(2 * Z):
-            tail_send[k, i] = part[i * ROOM : (i + 1) * ROOM]
-        for i in range(Z, 2 * Z):
+        last_send[:, columns[k]] = part[: Z * ROOM]
+        for i in range(Z):
+            tail_send[k, i] = part[(Z + i) * ROOM : (Z + i + 1) * ROOM]
             send_tail(k, i)
 
     total = total_y[...]
@@ -279,25 +282,29 @@
     high = total.astype(BF16)
     low = (total - high.astype(F32)).astype(BF16)
     exact = dot(onto, high) + dot(onto, low)
-    for i in range(Z):
-        for k in range(CHUNKS):
-            rows = exact[i * ROOM : (i + 1) * ROOM, k * CHUNK : (k + 1) * CHUNK]
-            tail_send[k, i] = tail_send[k, i] - rows
-            if i > 0:
-                send_tail(k, i)
-
+    last_send[...] = last_send[...] - exact
+    move_last = {}
+    for i in range(1, Z):
+        rows = pl.ds(i * ROOM, ROOM)
+        move_last[i] = send(last_send.at[rows, :], last_recv.at[rows, :], tail_peer(i))
+
+    for copy in sent:
+        copy.wait_send()
     for k in range(CHUNKS):
-        part = tail_send[k, 0]
-        for i in range(1, 2 * Z):
+        part = last_send[:ROOM, columns[k]]
+        for i in range(Z):
             move_tail[k, i].wait_recv()
             part = part + tail_recv[k, i]
-        out[:, columns[k]] = part[:SAMP]
-    for copy in sent:
-        copy.wait_send()
+        total_y[:ROOM, columns[k]] = part
+    part = total_y[:ROOM, :]
+    for i in range(1, Z):
+        move_last[i].wait_recv()
+        part = part + last_recv[i * ROOM : (i + 1) * ROOM, :]
+    out[...] = part[:SAMP]
 
 
 LOCAL = 3 + 8 + Z * X
-REMOTE = 1 + 3 * CHUNKS + 4 + 3 + 3 + 4 + (2 * Z - 1) * CHUNKS
+REMOTE = 1 + 3 * CHUNKS + 4 + 3 + 3 + 4 + Z * CHUNKS + Z - 1
 
 
 def per_device(vectors, leaf_in, leaf_out, factors, dense_rows, sample_rows):
@@ -334,8 +341,10 @@
         vmem((8 * ROOM, RANK), BF16),
         vmem((8 * ROOM, RANK), BF16),
         vmem((16 * ROOM, RANK), BF16),
-        vmem((CHUNKS, 2 * Z, ROOM, CHUNK), F32),
-        vmem((CHUNKS, 2 * Z, ROOM, CHUNK), F32),
+        vmem((CHUNKS, Z, ROOM, CHUNK), F32),
+        vmem((CHUNKS, Z, ROOM, CHUNK), F32),
+        vmem((Z * ROOM, VECS), F32),
+        vmem((Z * ROOM, VECS), F32),
         pltpu.SemaphoreType.DMA((LOCAL,)),
         pltpu.SemaphoreType.DMA((REMOTE,)),
         pltpu.SemaphoreType.DMA((REMOTE,)),

time: 38.1 us -> 37 us (0.971)
  Pallas kernels: 36.5 us -> 35.5 us
    pallas_call x1, Pallas kernels: 36.5 us -> 35.5 us  [per_device(): pl.pallas_call(kernel, out_shape=jax.ShapeDtypeStruct((SAMP, VECS), F32),...]
where the time goes in v3:
time: 37 us; the launch traced here: 36.8 us
  Pallas kernels  35.5 us (96%)
  local copies, waits for them, and re-layouts  1.31 us (4%)
    pallas_call x1, Pallas kernels, per_device(): pl.pallas_call(kernel, out_shape=jax.ShapeDtypeStruct((SAMP, VECS), F32),...  35.5 us
    unnamed x1, local copies, waits for them, and re-layouts  1.31 us

profile of v3, /device:TPU:8, one launch (start us, length us, event | category | flops | bytes accessed | tf_op | source)
XLA Modules:
  0.0 36.8 jit_solution(1133929588089968517)
XLA Ops:
  0.0 35.5 %shard_map.64 = f32[6,384]{1,0:T(8,128)} custom-call(s32[6]{0:T(128)} %samp.1, bf16[2048,384]{1,0:T(8,128)(2,1)} %vec_hbm.1, bf16[256,2048]{1,0:T(8,128)(2,1)} %lin_hbm.1, bf16[2048,256]{1,0:T(8,128)(2,1)} %lout_hbm.1, bf16[1,8,2,256,256]{4,3,2,1,0:T(8,128)(2,1)} %fac_hbm.1, bf16[1536,2048]{1,0:T(8,128)(2,1)} %dense_hbm.1), custom_call_target="tpu_custom_call" | custom-call | flops 3400000000 | bytes 12582912 | tf_op jit(solution)/shard_map/pallas_call | solution.py:353
  35.5 1.3 %copy.8 = f32[6,384]{1,0:T(8,128)} copy(f32[6,384]{1,0:T(8,128)} %shard_map.64) | data formatting | bytes 18432

commit v4 on v3

--- a/solution.py
+++ b/solution.py
@@ -61,12 +61,12 @@
 
 
 def kernel(
-    samp, vec_hbm, lin_hbm, lout_hbm, fac_hbm, dense_hbm, out,
+    samp_hbm, vec_hbm, lin_hbm, lout_hbm, fac_hbm, dense_hbm, out,
     vec, lin, lout, fac, dense, perm,
     c0_send, c0_recv, c1, c1_recv, c2, c2_recv, c3, c3_recv,
     half_send, half_recv, mine, xs_send, xs_recv, ys_send, ys_recv, total_y,
     w_send4, w_recv4, w_send2, w_recv2, w_send1, w_recv1, w_send_x, w_recv_x, w_all,
-    tail_send, tail_recv, last_send, last_recv, local_sem, send_sem, recv_sem,
+    tail_send, tail_recv, last_send, last_recv, samp, local_sem, send_sem, recv_sem,
 ):
     z, lvl = lax.axis_index("grp"), lax.axis_index("lvl")
     x, y, core = lvl // 8, (lvl // 2) % 4, lvl % 2
@@ -127,6 +127,7 @@
             )
         return copies
 
+    got_samp = load(samp_hbm, samp)
     got_lin, got_vec = load(lin_hbm, lin), load(vec_hbm, vec)
     got_lout = load(lout_hbm, lout)
     got_fac = {7: load_factors(7)}
@@ -142,13 +143,14 @@
     for level in (2, 5, 3, 4):
         got_fac[level] = load_factors(level)
 
+    perm[...] = permutation(core, y)
+    got_samp.wait()
     column = lax.broadcasted_iota(jnp.int32, (2 * ROOM, ROWS), 1)
     row = lax.broadcasted_iota(jnp.int32, (2 * ROOM, ROWS), 0)
     hot = jnp.zeros((2 * ROOM, ROWS), F32)
     for i in range(SAMP):
         hot = jnp.where((row == i) & (column == samp[i]), 1.0, hot)
     hot = hot.astype(BF16)
-    perm[...] = permutation(core, y)
 
     got_lin.wait()
     got_vec.wait()
@@ -303,7 +305,7 @@
     out[...] = part[:SAMP]
 
 
-LOCAL = 3 + 8 + Z * X
+LOCAL = 4 + 8 + Z * X
 REMOTE = 1 + 3 * CHUNKS + 4 + 3 + 3 + 4 + Z * CHUNKS + Z - 1
 
 
@@ -345,6 +347,7 @@
         vmem((CHUNKS, Z, ROOM, CHUNK), F32),
         vmem((Z * ROOM, VECS), F32),
         vmem((Z * ROOM, VECS), F32),
+        pltpu.SMEM((SAMP,), jnp.int32),
         pltpu.SemaphoreType.DMA((LOCAL,)),
         pltpu.SemaphoreType.DMA((REMOTE,)),
         pltpu.SemaphoreType.DMA((REMOTE,)),
@@ -352,8 +355,8 @@
     anywhere = pl.BlockSpec(memory_space=pl.ANY)
     return pl.pallas_call(
         kernel,
-        out_shape=jax.ShapeDtypeStruct((SAMP, VECS), F32),
-        in_specs=[pl.BlockSpec(memory_space=pltpu.SMEM)] + [anywhere] * 5,
+        out_shape=pltpu.VMEM((SAMP, VECS), F32),
+        in_specs=[anywhere] * 6,
         out_specs=pl.BlockSpec(memory_space=pltpu.VMEM),
         scratch_shapes=scratch,
         compiler_params=pltpu.CompilerParams(

time: 37 us -> 34.7 us (0.938)
  Pallas kernels: 35.5 us -> 34.1 us
  local copies, waits for them, and re-layouts: 1.31 us -> 0.6 us
    pallas_call x1, Pallas kernels: 35.5 us -> 34.1 us  [per_device(): pl.pallas_call(kernel, out_shape=pltpu.VMEM((SAMP, VECS), F32), in_specs=...]
    unnamed x1, local copies, waits for them, and re-layouts: 1.31 us -> 0.6 us
where the time goes in v4:
time: 34.7 us
  Pallas kernels  34.1 us (98%)
  local copies, waits for them, and re-layouts  0.6 us (2%)
    pallas_call x1, Pallas kernels, per_device(): pl.pallas_call(kernel, out_shape=pltpu.VMEM((SAMP, VECS), F32), in_specs=...  34.1 us

profile of v4, /device:TPU:8, one launch (start us, length us, event | category | flops | bytes accessed | tf_op | source)
XLA Modules:
  0.0 34.7 jit_solution(10518578632891164569)
XLA Ops:
  0.0 34.1 %shard_map.64 = f32[6,384]{1,0:T(8,128)S(1)} custom-call(s32[6]{0:T(128)} %samp_hbm.1, bf16[2048,384]{1,0:T(8,128)(2,1)} %vec_hbm.1, bf16[256,2048]{1,0:T(8,128)(2,1)} %lin_hbm.1, bf16[2048,256]{1,0:T(8,128)(2,1)} %lout_hbm.1, bf16[1,8,2,256,256]{4,3,2,1,0:T(8,128)(2,1)} %fac_hbm.1, bf16[1536,2048]{1,0:T(8,128)(2,1)} %dense_hbm.1), custom_call_target="tpu_custom_call" | custom-call | flops 3400000000 | bytes 12582912 | tf_op jit(solution)/shard_map/pallas_call | solution.py:356
  34.1 0.6 %copy.8 = f32[6,384]{1,0:T(8,128)} copy(f32[6,384]{1,0:T(8,128)S(1)} %shard_map.64) | data formatting | bytes 18432

commit v5 on v4

--- a/solution.py
+++ b/solution.py
@@ -118,12 +118,14 @@
     def load_factors(level):
         return load(fac_hbm.at[0, level], fac.at[level])
 
+    order = (2, 1, 3, 0)
+
     def load_dense(j):
         copies = []
         for group in range(Z):
             first = pl.multiple_of(group * (X * BLOCK) + (x ^ j) * BLOCK, BLOCK)
             copies.append(
-                load(dense_hbm.at[pl.ds(first, BLOCK), :], dense.at[j, pl.ds(group * BLOCK, BLOCK), :])
+                load(dense_hbm.at[pl.ds(first, BLOCK), :], dense.at[order.index(j), pl.ds(group * BLOCK, BLOCK), :])
             )
         return copies
 
@@ -133,7 +135,6 @@
     got_fac = {7: load_factors(7)}
     got_fac[0] = load_factors(0)
     got_dense = {}
-    order = (2, 1, 3, 0)
     for j in order[:2]:
         got_dense[j] = load_dense(j)
     got_fac[1] = load_factors(1)
@@ -166,16 +167,20 @@
     move4 = send(w_send4, w_recv4, z_peer(4))
     move_c0 = send(c0_send, c0_recv, core_peer())
 
-    def dense_product(j):
-        for copy in got_dense[j]:
-            copy.wait()
-        product = dot16(dense[j], vec[...])
-        product = dot(perm[...], product)
-        mine[j] = product[:HALF]
-        half_send[j] = product[HALF:].astype(BF16)
-        return send(half_send.at[j], half_recv.at[j], core_peer())
-
-    move_half = {2: dense_product(2)}
+    def dense_products(first, blocks):
+        for j in blocks:
+            for copy in got_dense[j]:
+                copy.wait()
+        rows = dense[first : first + len(blocks)].reshape(len(blocks) * 2 * HALF, ROWS)
+        products = dot16(rows, vec[...])
+        for i, j in enumerate(blocks):
+            product = dot(perm[...], products[i * 2 * HALF : (i + 1) * 2 * HALF])
+            mine[j] = product[:HALF]
+            half_send[j] = product[HALF:].astype(BF16)
+            move_half[j] = send(half_send.at[j], half_recv.at[j], core_peer())
+
+    move_half = {}
+    dense_products(0, (2,))
     got_fac[0].wait()
     near = dot(fac[0, 0], c0_send[...])
     move_c0.wait_recv()
@@ -199,11 +204,10 @@
 
     move_c1 = [exchange(k, c1, c1_recv, y_peer(1)) for k in range(CHUNKS)]
     move_xs, move_c2, move_c3 = {}, {}, {}
-    move_half[1] = dense_product(1)
+    dense_products(1, (1, 3))
     move_xs[2] = send_half(2)
-    move_half[3] = dense_product(3)
+    dense_products(3, (0,))
     move_xs[1] = send_half(1)
-    move_half[0] = dense_product(0)
     move_xs[3] = send_half(3)
 
     got_fac[1].wait()

time: 34.7 us -> 34.7 us (level)
  no operation moved by 1% of the time
where the time goes in v5:
time: 34.7 us
  Pallas kernels  34 us (98%)
  local copies, waits for them, and re-layouts  0.6 us (2%)
    pallas_call x1, Pallas kernels, per_device(): pl.pallas_call(kernel, out_shape=pltpu.VMEM((SAMP, VECS), F32), in_specs=...  34 us

profile of v5, /device:TPU:8, one launch (start us, length us, event | category | flops | bytes accessed | tf_op | source)
XLA Modules:
  0.0 34.7 jit_solution(9789571939614442440)
XLA Ops:
  0.0 34.0 %shard_map.64 = f32[6,384]{1,0:T(8,128)S(1)} custom-call(s32[6]{0:T(128)} %samp_hbm.1, bf16[2048,384]{1,0:T(8,128)(2,1)} %vec_hbm.1, bf16[256,2048]{1,0:T(8,128)(2,1)} %lin_hbm.1, bf16[2048,256]{1,0:T(8,128)(2,1)} %lout_hbm.1, bf16[1,8,2,256,256]{4,3,2,1,0:T(8,128)(2,1)} %fac_hbm.1, bf16[1536,2048]{1,0:T(8,128)(2,1)} %dense_hbm.1), custom_call_target="tpu_custom_call" | custom-call | flops 3400000000 | bytes 12582912 | tf_op jit(solution)/shard_map/pallas_call | solution.py:360
  34.0 0.6 %copy.8 = f32[6,384]{1,0:T(8,128)} copy(f32[6,384]{1,0:T(8,128)S(1)} %shard_map.64) | data formatting | bytes 18432
